TPU v7x, 32 devices: a whole 2x2x4 slice. The times are simulated.
32 devices in a mesh: row: 4 (over x, core), col: 8 (over z, y).
Axes of the slice: x: 2, y: 2, z: 4, core: 2. Of those that a mesh axis runs over, the one named last changes fastest.
Arguments:
- hamiltonian_blocks: float32 [4, 8, 320, 128, 128], P('row', 'col'), may hold values from -0.0625 to 0.0625
- block_vectors: float32 [16, 32768], P(None, ('row', 'col')), may hold values from -6 to 6
- row_list: int32 [4, 8, 320], P('row', 'col'), may hold values from 0 to 63, as said below
- col_list: int32 [4, 8, 320], P('row', 'col'), may hold values from 0 to 31, as said below
- counts: int32 [4, 8], P('row', 'col'), may hold values from 1 to 320, as said below
Outputs:
- image_vectors: float32 [16, 32768], P(None, ('row', 'col'))
Inputs may be any that keep to these rules, and one draw needn't show every extreme that they name: row_list gives a block row within the tile row, at least that of the tile's column block for blocks on the tile's own diagonal segment; every tile has a slot at the last block row. col_list of tile (r, c) names only column blocks of segments with row index at most r, so stored blocks lie on or below the block diagonal; the last tile row reaches the last column block. The live slots of a tile are its first counts slots; tiles of the last tile row are full and the count grows with the tile row.
All inputs are finite; a program needn't handle non-finite values.
Results may differ from a plain program's by a relative error of at most 0.0003.
Values sent between devices are 32-bit elements; how exact they have to be, the bound alone decides.
A program may use at most 128 MiB of HBM per device.

v0:
```python
import jax
import jax.numpy as jnp
from jax import lax
from jax.sharding import PartitionSpec as P

SB = 8


def accumulate(sums_pair, blocks, row_index, col_index, live_mask, source_rows, source_cols):
    direct_sum, mirror_sum = sums_pair
    col_vectors = source_cols[:, col_index, :]
    row_vectors = source_rows[:, row_index, :]
    direct = (
        jnp.einsum("kpb,pab->kpa", col_vectors, blocks, precision=lax.Precision.HIGHEST)
        * live_mask[None, :, None]
    )
    mirror = (
        jnp.einsum("kpa,pab->kpb", row_vectors, blocks, precision=lax.Precision.HIGHEST)
        * live_mask[None, :, None]
    )
    return (direct_sum.at[:, row_index, :].add(direct), mirror_sum.at[:, col_index, :].add(mirror))


def tile_products(blocks, row_index, col_index, tile_count, source_rows, source_cols):
    width = source_rows.shape[2]
    slot_total = blocks.shape[0]
    sums_pair = (
        jnp.zeros((source_rows.shape[0], source_rows.shape[1], width), jnp.float32),
        jnp.zeros((source_cols.shape[0], source_cols.shape[1], width), jnp.float32),
    )
    live_mask = (jnp.arange(slot_total, dtype=jnp.int32) < tile_count).astype(jnp.float32)
    return accumulate(sums_pair, blocks, row_index, col_index, live_mask, source_rows, source_cols)


def local(hamiltonian_blocks, block_vectors, row_list, col_list, counts):
    blocks = hamiltonian_blocks[0, 0]
    row_slots = row_list[0, 0]
    col_slots = col_list[0, 0]
    tile_count = counts[0, 0]
    vec_count = block_vectors.shape[0]
    width = blocks.shape[1]
    rows_axis = lax.axis_size("row")
    cols_axis = lax.axis_size("col")
    tile_row = lax.axis_index("row")
    tile_col = lax.axis_index("col")
    everything = lax.all_gather(block_vectors, ("row", "col"), axis=1, tiled=True)
    source = everything.reshape(vec_count, rows_axis * cols_axis * SB, width)
    global_row = row_slots + tile_row * cols_axis * SB
    global_col = col_slots // SB * cols_axis * SB + tile_col * SB + col_slots % SB
    direct_sum, mirror_sum = tile_products(
        blocks, global_row, global_col, tile_count, source, source
    )
    combined = (direct_sum + mirror_sum).reshape(vec_count, rows_axis * cols_axis * SB * width)
    return lax.psum_scatter(combined, ("row", "col"), scatter_dimension=1, tiled=True)


def solution(mesh):
    return jax.shard_map(
        local,
        mesh=mesh,
        in_specs=(
            P("row", "col", None, None, None),
            P(None, ("row", "col")),
            P("row", "col", None),
            P("row", "col", None),
            P("row", "col"),
        ),
        out_specs=P(None, ("row", "col")),
        check_vma=False,
    )
```

profile of v0, /device:TPU:0, one launch (start us, length us, event | category | flops | bytes accessed | tf_op | source)
XLA Modules:
  0.0 343.8 jit_solution(5980570360441181232)
XLA Ops:
  6.5 0.0 all-gather.2.cloned.1.call-start
  6.5 0.7 all-gather.2.cloned.1.call-update
  7.3 0.0 reduce-scatter.2.cloned.1.call-start
  8.0 0.7 fusion.18
  8.7 0.7 fusion.19
  9.4 60.3 %all-gather.2.cloned.1.call-done = f32[16,32768]{1,0:T(8,128)} async-done(((f32[16,1024]{1,0:T(8,128)}), f32[16,32768]{1,0:T(8,128)}) %all-gather.2.cloned.1.call-update) | async-done | bytes 2097168 | tf_op jit(solution)/shard_map/all_gather | solution.py:46
  69.7 1.7 copy_bitcast_fusion.1
  71.5 2.7 gather_fusion.1
  74.1 2.6 gather_fusion
  76.8 0.0 copy-start
  76.8 20.9 %fusion.11 = f32[320,16,128]{2,1,0:T(8,128)S(1)} fusion(f32[1,1,320,128,128]{4,3,2,1,0:T(8,128)} %param.5, f32[320,16,128]{2,1,0:T(8,128)} %gather_fusion.1, f32[320]{0:T(512)S(1)} %fusion.16), kind=kOutput, calls=%fused_computation.14 | convolution fusion | flops 1007288320 | bytes 26215680 | tf_op jit(solution)/shard_map/kpa,pab->kpb/dot_general | solution.py:18
  97.6 0.0 copy-done
  97.7 36.2 %fusion.6 = f32[320,16,128]{2,1,0:T(8,128)} fusion(f32[1,1,320,128,128]{4,3,2,1,0:T(8,128)} %param.5, f32[320,16,128]{2,1,0:T(8,128)S(1)} %copy-done, f32[320]{0:T(512)S(1)} %fusion.16), kind=kOutput, calls=%fused_computation.13 | convolution fusion | flops 1007288320 | bytes 26215680 | tf_op jit(solution)/shard_map/kpb,pab->kpa/dot_general | solution.py:14
  133.9 1.4 broadcast.142.clone.1
  135.3 35.8 %scatter_fusion.1 = f32[16,256,128]{2,0,1:T(8,128)} fusion(f32[16,256,128]{2,0,1:T(8,128)} %broadcast.142.clone.1, s32[320]{0:T(512)S(1)} %fusion.19, f32[320,16,128]{2,1,0:T(8,128)S(1)} %fusion.11), kind=kCustom, calls=%fused_computation.3 | custom fusion | flops 655360 | bytes 7865600 | tf_op jit(solution)/shard_map/scatter-add | solution.py:21
  171.1 0.1 broadcast.142.clone
  171.3 25.6 %scatter_fusion = f32[16,256,128]{2,0,1:T(8,128)S(1)} fusion(f32[16,256,128]{2,0,1:T(8,128)S(1)} %broadcast.142.clone, s32[320]{0:T(512)S(1)} %fusion.18, f32[320,16,128]{2,1,0:T(8,128)} %fusion.6), kind=kCustom, calls=%fused_computation.2 | custom fusion | flops 655360 | bytes 7865600 | tf_op jit(solution)/shard_map/scatter-add | solution.py:21
  196.8 3.2 copy_bitcast_fusion
  200.0 0.0 reduce-scatter.2.cloned.1.call-update
  200.0 136.9 %reduce-scatter.2.cloned.1.call-done = f32[16,1024]{1,0:T(8,128)} async-done(((f32[16,32768]{1,0:T(8,128)}), f32[16,1024]{1,0:T(8,128)}) %reduce-scatter.2.cloned.1.call-update) | async-done | bytes 65552 | tf_op jit(solution)/shard_map/reduce_scatter | solution.py:54
  (3 shorter events, 0.0 us)
Async XLA Ops:
  6.5 63.2 %all-gather.2.cloned.1.call-start = ((), (), s32[]{:S(2)}) async-start(), calls=%async_computation.1 | async-start | bytes 2162688 | tf_op jit(solution)/shard_map/all_gather | solution.py:46
  7.3 329.7 %reduce-scatter.2.cloned.1.call-start = ((), (), s32[]{:S(2)}) async-start(), calls=%async_computation.2 | async-start | bytes 2162688 | tf_op jit(solution)/shard_map/reduce_scatter | solution.py:54
  76.8 20.9 %copy-start = (f32[320,16,128]{2,1,0:T(8,128)S(1)}, f32[320,16,128]{2,1,0:T(8,128)}, u32[]{:S(2)}) copy-start(f32[320,16,128]{2,1,0:T(8,128)} %gather_fusion) | copy-start | bytes 7864324
Sparse Core Ops, SparseCore 0:
  10.4 59.2 all-gather.1
  200.1 136.7 reduce-scatter.1
where the time goes:
time: 346 us; the launch traced here: 344 us
  waiting for transfers between devices  198 us (57%)
  other arithmetic  66 us (19%)
  matrix products  57.1 us (17%)
  between operations  14.1 us (4%)
  local copies, waits for them, and re-layouts  8.62 us (2%)
    reduce_scatter x1, waiting for transfers between devices, local(): lax.psum_scatter(combined, ('row', 'col'), scatter_dimension=1, tiled=True)  137 us
    all_gather x1, waiting for transfers between devices, local(): lax.all_gather(block_vectors, ('row', 'col'), axis=1, tiled=True)  60.3 us
    dot_general x1, matrix products, accumulate(): jnp.einsum('kpb,pab->kpa', col_vectors, blocks, precision=lax.Precision.H...  36.2 us
    scatter-add x1, other arithmetic, accumulate(): mirror_sum.at[:, col_index, :].add(mirror)  35.8 us
    scatter-add x1, other arithmetic, accumulate(): direct_sum.at[:, row_index, :].add(direct)  25.6 us
    dot_general x1, matrix products, accumulate(): jnp.einsum('kpa,pab->kpb', row_vectors, blocks, precision=lax.Precision.H...  20.9 us
  transfers between devices with their start and end apart: 2, of which 2 were waited for; matrix products, arithmetic and copies ran while one was open for 0% of the time, Pallas kernels for 0%

commit v1 on v0

v1 whole, which is shorter than its diff:
```python
import functools

import jax
import jax.numpy as jnp
from jax import lax
from jax.experimental import pallas as pl
from jax.experimental.pallas import tpu as pltpu
from jax.sharding import PartitionSpec as P

SB = 8


def split(x):
    high = x.astype(jnp.bfloat16)
    low = (x - high.astype(jnp.float32)).astype(jnp.bfloat16)
    return high, low


def split_rows(src, dst, vec):
    def body(t, _):
        high, low = split(src[t])
        dst[t, 0:vec, :] = high
        dst[t, vec : 2 * vec, :] = low
        return 0

    lax.fori_loop(0, src.shape[0], body, 0)


def products_kernel(chunk, unroll, rows, cols, counts, blocks, xr, xc, acc_d, acc_m, sr, sc):
    step = pl.program_id(0)
    vec = xr.shape[1]
    width = xr.shape[2]

    @pl.when(step == 0)
    def _():
        acc_d[...] = jnp.zeros_like(acc_d)
        acc_m[...] = jnp.zeros_like(acc_m)
        split_rows(xr, sr, vec)
        split_rows(xc, sc, vec)

    live = counts[0]

    def group(g, _):
        results = []
        for u in range(unroll):
            slot = g * unroll + u
            k = step * chunk + slot
            i = rows[k]
            j = cols[k]
            high, low = split(blocks[slot])
            d = lax.dot_general(
                sc[j],
                jnp.concatenate([high, low], axis=0),
                (((1,), (1,)), ((), ())),
                preferred_element_type=jnp.float32,
            )
            m = lax.dot_general(
                sr[i],
                jnp.concatenate([high, low], axis=1),
                (((1,), (0,)), ((), ())),
                preferred_element_type=jnp.float32,
            )
            mask = jnp.where(k < live, 1.0, 0.0).astype(jnp.float32)
            fold = [
                (z[0:vec, 0:width] + (z[vec : 2 * vec, 0:width] + z[0:vec, width:])) * mask for z in (d, m)
            ]
            results.append((i, j, fold[0], fold[1]))
        for i, j, d, m in results:
            acc_d[i] = acc_d[i] + d
            acc_m[j] = acc_m[j] + m
        return 0

    groups = jnp.clip(pl.cdiv(live - step * chunk, unroll), 0, chunk // unroll)
    lax.fori_loop(0, groups, group, 0)


def products(blocks, xr, xc, rows, cols, counts):
    cap, width, _ = blocks.shape
    vec = xr.shape[1]
    chunk = 32 if cap % 32 == 0 else cap
    unroll = 8 if chunk % 8 == 0 else 1
    whole = lambda shape: pl.BlockSpec(shape, lambda s, *_: (0, 0, 0))
    return pl.pallas_call(
        functools.partial(products_kernel, chunk, unroll),
        grid_spec=pltpu.PrefetchScalarGridSpec(
            num_scalar_prefetch=3,
            grid=(cap // chunk,),
            in_specs=[
                pl.BlockSpec((chunk, width, width), lambda s, *_: (s, 0, 0)),
                whole(xr.shape),
                whole(xc.shape),
            ],
            out_specs=[whole(xr.shape), whole(xc.shape)],
            scratch_shapes=[
                pltpu.VMEM((xr.shape[0], 2 * vec, width), jnp.bfloat16),
                pltpu.VMEM((xc.shape[0], 2 * vec, width), jnp.bfloat16),
            ],
        ),
        out_shape=[
            jax.ShapeDtypeStruct(xr.shape, jnp.float32),
            jax.ShapeDtypeStruct(xc.shape, jnp.float32),
        ],
        compiler_params=pltpu.CompilerParams(vmem_limit_bytes=40 * 2**20),
    )(rows, cols, counts, blocks, xr, xc)


def local(hamiltonian_blocks, block_vectors, row_list, col_list, counts):
    blocks = hamiltonian_blocks[0, 0]
    vec, states = block_vectors.shape
    width = blocks.shape[1]
    own = block_vectors.reshape(vec, SB, width).transpose(1, 0, 2)
    xr = lax.all_gather(own, "col", axis=0, tiled=True)
    xc = lax.all_gather(own, "row", axis=0, tiled=True)
    direct, mirror = products(blocks, xr, xc, row_list[0, 0], col_list[0, 0], counts[0])
    total = lax.psum_scatter(direct, "col", scatter_dimension=0, tiled=True)
    total = total + lax.psum_scatter(mirror, "row", scatter_dimension=0, tiled=True)
    return total.transpose(1, 0, 2).reshape(vec, states)


def solution(mesh):
    return jax.shard_map(
        local,
        mesh=mesh,
        in_specs=(
            P("row", "col", None, None, None),
            P(None, ("row", "col")),
            P("row", "col", None),
            P("row", "col", None),
            P("row", "col"),
        ),
        out_specs=P(None, ("row", "col")),
        check_vma=False,
    )
```

time: 346 us -> 161 us (0.47)
  waiting for transfers between devices: 198 us -> 90.2 us
  other arithmetic: 66 us -> 2.91 us
  matrix products: 57.1 us -> 0 us
  blocking collectives: 0 us -> 39.1 us
  Pallas kernels: 0 us -> 13.6 us
  local copies, waits for them, and re-layouts: 8.62 us -> 0.87 us
    scatter-add x2 -> x0, other arithmetic: 61.4 us -> none  [the longest x1 35.8 us: accumulate(): mirror_sum.at[:, col_index, :].add(mirror)]
    all_gather x1 -> x0, waiting for transfers between devices: 60.3 us -> none  [local(): lax.all_gather(block_vectors, ('row', 'col'), axis=1, tiled=True)]
    dot_general x2 -> x0, matrix products: 57.1 us -> none  [the longest x1 36.2 us: accumulate(): jnp.einsum('kpb,pab->kpa', col_vectors, blocks, precision=lax.Precision.H...]
    reduce_scatter x1 -> x2, waiting for transfers between devices: 137 us -> 89.5 us  [the longest x1 66.1 us: local(): total = lax.psum_scatter(direct, 'col', scatter_dimension=0, tiled=True)]
    all_gather x0 -> x2, blocking collectives: none -> 39.1 us  [the longest x1 31.9 us: local(): xr = lax.all_gather(own, 'col', axis=0, tiled=True)]
    pallas_call x0 -> x1, Pallas kernels: none -> 13.6 us  [products(): pl.pallas_call(functools.partial(products_kernel, chunk, unroll), grid_sp...]
    gather x2 -> x0, local copies, waits for them, and re-layouts: 5.28 us -> none  [the longest x1 2.66 us: accumulate(): row_vectors = source_rows[:, row_index, :]]
where the time goes in v1:
time: 161 us
  waiting for transfers between devices  90.2 us (56%)
  blocking collectives  39.1 us (24%)
  between operations  14.1 us (9%)
  Pallas kernels  13.6 us (8%)
  other arithmetic  2.91 us (2%)
    reduce_scatter x1, waiting for transfers between devices, local(): total = lax.psum_scatter(direct, 'col', scatter_dimension=0, tiled=True)  66.1 us
    all_gather x1, blocking collectives, local(): xr = lax.all_gather(own, 'col', axis=0, tiled=True)  31.9 us
    reduce_scatter x1, waiting for transfers between devices, local(): lax.psum_scatter(mirror, 'row', scatter_dimension=0, tiled=True)  23.4 us
    pallas_call x1, Pallas kernels, products(): pl.pallas_call(functools.partial(products_kernel, chunk, unroll), grid_sp...  13.6 us
    all_gather x1, blocking collectives, local(): xc = lax.all_gather(own, 'row', axis=0, tiled=True)  7.19 us
  transfers between devices with their start and end apart: 2, of which 2 were waited for; matrix products, arithmetic and copies ran while one was open for 0% of the time, Pallas kernels for 0%

profile of v1, /device:TPU:0, one launch (start us, length us, event | category | flops | bytes accessed | tf_op | source)
XLA Modules:
  0.0 160.8 jit_solution(16207876125733088907)
XLA Ops:
  6.5 0.0 reduce-scatter.5.cloned.1.call-start
  6.5 0.9 copy.12
  7.4 7.2 %all_gather.7.xc = f32[32,16,128]{2,1,0:T(8,128)S(1)} all-gather(f32[8,16,128]{2,1,0:T(8,128)S(1)} %copy.8), channel_id=1, replica_groups=mesh['row'=4,'col'=8] {'row'}, dimensions={0}, use_global_device_ids=true | all-gather | bytes 327680 | tf_op jit(solution)/shard_map/all_gather | solution.py:113
  14.6 31.9 %all_gather.6.xr = f32[64,16,128]{2,1,0:T(8,128)S(1)} all-gather(f32[8,16,128]{2,1,0:T(8,128)S(1)} %copy.8), channel_id=1, replica_groups=mesh['row'=4,'col'=8] {'col'}, dimensions={0}, use_global_device_ids=true | all-gather | bytes 589824 | tf_op jit(solution)/shard_map/all_gather | solution.py:112
  47.2 0.7 reduce.rows
  47.9 0.7 reduce.1.cols
  48.6 13.6 %shard_map.55 = (f32[64,16,128]{2,1,0:T(8,128)}, f32[32,16,128]{2,1,0:T(8,128)}) custom-call(s32[320]{0:T(512)S(1)} %reduce.rows, s32[320]{0:T(512)S(1)} %reduce.1.cols, s32[1]{0:T(128)} %bitcast.12.counts, f32[320,128,128]{2,1,0:T(8,128)} %bitcast.13, f32[64,16,128]{2,1,0:T(8,128)S(1)} %all_gather.6.xr, f32[32,16,128]{2,1,0:T(8,128)S(1)} %all_gather.7.xc), custom_call_target="tpu_custom_call" | custom-call | tf_op jit(solution)/shard_map/pallas_call | solution.py:83
  62.2 0.0 reduce-scatter.5.cloned.1.call-update
  62.2 0.0 reduce-scatter.3.cloned.1.call-start
  62.2 0.7 reduce-scatter.3.cloned.1.call-update
  63.0 23.4 %reduce-scatter.5.cloned.1.call-done = f32[8,16,128]{2,1,0:T(8,128)} async-done(((f32[32,16,128]{2,1,0:T(8,128)}), f32[8,16,128]{2,1,0:T(8,128)}) %reduce-scatter.5.cloned.1.call-update) | async-done | bytes 65552 | tf_op jit(solution)/shard_map/reduce_scatter | solution.py:116
  86.4 66.1 %reduce-scatter.3.cloned.1.call-done = f32[8,16,128]{2,1,0:T(8,128)} async-done(((f32[64,16,128]{2,1,0:T(8,128)}), f32[8,16,128]{2,1,0:T(8,128)}) %reduce-scatter.3.cloned.1.call-update) | async-done | bytes 65552 | tf_op jit(solution)/shard_map/reduce_scatter | solution.py:115
  152.5 1.5 copy_bitcast_fusion
  (1 shorter events, 0.0 us)
Async XLA Ops:
  6.5 79.8 %reduce-scatter.5.cloned.1.call-start = ((), (), s32[]{:S(2)}) async-start(), calls=%async_computation.3 | async-start | bytes 327680 | tf_op jit(solution)/shard_map/reduce_scatter | solution.py:116
  62.2 90.3 %reduce-scatter.3.cloned.1.call-start = ((), (), s32[]{:S(2)}) async-start(), calls=%async_computation.2 | async-start | bytes 589824 | tf_op jit(solution)/shard_map/reduce_scatter | solution.py:115
Sparse Core Ops, SparseCore 0:
  62.3 24.0 reduce-scatter.4
  90.1 62.3 reduce-scatter.2

commit v2 on v1

--- a/solution.py
+++ b/solution.py
@@ -104,17 +104,176 @@
     )(rows, cols, counts, blocks, xr, xc)
 
 
+MESH = pl.DeviceIdType.MESH
+
+
+def places(n_row, n_col):
+    r = lax.axis_index("row")
+    c = lax.axis_index("col")
+    inner = 2 if n_col % 2 == 0 else 1
+    return r, c, c // inner, c % inner, inner, n_col // inner
+
+
+def greet(n_row, n_col):
+    r, c, hi, lo, inner, outer = places(n_row, n_col)
+    barrier = pltpu.get_barrier_semaphore()
+    met = 0
+    for d in range(1, n_row):
+        pl.semaphore_signal(barrier, inc=1, device_id=(lax.rem(r + d, n_row), c), device_id_type=MESH)
+        met += 1
+    for d in range(1, outer):
+        pl.semaphore_signal(
+            barrier, inc=1, device_id=(r, lax.rem(hi + d, outer) * inner + lo), device_id_type=MESH
+        )
+        met += 1
+    for e in range(1, inner):
+        pl.semaphore_signal(
+            barrier, inc=1, device_id=(r, hi * inner + lax.rem(lo + e, inner)), device_id_type=MESH
+        )
+        met += 1
+    pl.semaphore_wait(barrier, met)
+
+
+def remote(src, dst, send, recv, device):
+    return pltpu.make_async_remote_copy(
+        src_ref=src, dst_ref=dst, send_sem=send, recv_sem=recv, device_id=device, device_id_type=MESH
+    )
+
+
+def gather_kernel(n_row, n_col, vectors, xr, xc, own, z_s, z_r, y_s, y_r, r_s, r_r):
+    r, c, hi, lo, inner, outer = places(n_row, n_col)
+    width = own.shape[2]
+    for t in range(SB):
+        own[t] = vectors[:, t * width : (t + 1) * width]
+    greet(n_row, n_col)
+    mate = hi * inner + (inner - 1 - lo)
+    piece = lambda ref, q: ref.at[pl.ds(q * SB, SB)]
+    started = []
+
+    def start(*a):
+        copy = remote(*a)
+        copy.start()
+        started.append(copy)
+
+    for d in range(1, outer):
+        start(own, piece(xr, c), z_s.at[d], z_r.at[d], (r, lax.rem(hi + d, outer) * inner + lo))
+    if inner == 2:
+        start(own, piece(xr, c), y_s.at[0], y_r.at[0], (r, mate))
+    for d in range(1, n_row):
+        start(own, piece(xc, r), r_s.at[d], r_r.at[d], (lax.rem(r + d, n_row), c))
+    xr[pl.ds(c * SB, SB)] = own[...]
+    xc[pl.ds(r * SB, SB)] = own[...]
+    for d in range(1, outer):
+        source = piece(xr, lax.rem(hi - d + outer, outer) * inner + lo)
+        remote(source, source, z_s.at[d], z_r.at[d], (r, mate)).wait_recv()
+        if inner == 2:
+            start(source, source, y_s.at[d], y_r.at[d], (r, mate))
+    if inner == 2:
+        for d in range(outer):
+            source = piece(xr, lax.rem(hi - d + outer, outer) * inner + 1 - lo)
+            remote(source, source, y_s.at[d], y_r.at[d], (r, mate)).wait_recv()
+    for d in range(1, n_row):
+        source = piece(xc, lax.rem(r - d + n_row, n_row))
+        remote(source, source, r_s.at[d], r_r.at[d], (lax.rem(r + d, n_row), c)).wait_recv()
+    for copy in started:
+        copy.wait_send()
+
+
+def scatter_kernel(n_row, n_col, direct, mirror, out, y_buf, z_out, z_buf, r_buf, z_s, z_r, y_s, y_r, r_s, r_r):
+    r, c, hi, lo, inner, outer = places(n_row, n_col)
+    width = direct.shape[2]
+    greet(n_row, n_col)
+    mate = hi * inner + (inner - 1 - lo)
+    started = []
+
+    def start(*a):
+        copy = remote(*a)
+        copy.start()
+        started.append(copy)
+        return copy
+
+    part = lambda ref, q: ref.at[pl.ds(q * SB, SB)]
+    to_mate = {}
+    order = list(range(1, outer)) + [0]
+    if inner == 2:
+        for d in order:
+            q = lax.rem(hi + d, outer) * inner + 1 - lo
+            to_mate[d] = start(part(direct, q), y_buf.at[d], y_s.at[d], y_r.at[d], (r, mate))
+    across = [
+        start(part(mirror, lax.rem(r + d, n_row)), r_buf.at[d], r_s.at[d], r_r.at[d], (lax.rem(r + d, n_row), c))
+        for d in range(1, n_row)
+    ]
+    along = []
+    for d in range(1, outer):
+        q = lax.rem(hi + d, outer) * inner + lo
+        mine = direct[pl.ds(q * SB, SB)]
+        if inner == 2:
+            to_mate[d].wait_recv()
+            mine = mine + y_buf[d]
+        z_out[d] = mine
+        along.append(start(z_out.at[d], z_buf.at[d], z_s.at[d], z_r.at[d], (r, q)))
+    total = direct[pl.ds(c * SB, SB)] + mirror[pl.ds(r * SB, SB)]
+    for d in range(1, n_row):
+        across[d - 1].wait_recv()
+        total = total + r_buf[d]
+    if inner == 2:
+        to_mate[0].wait_recv()
+        total = total + y_buf[0]
+    for d in range(1, outer):
+        along[d - 1].wait_recv()
+        total = total + z_buf[d]
+    for t in range(SB):
+        out[:, t * width : (t + 1) * width] = total[t]
+    for copy in started:
+        copy.wait_send()
+
+
+def semaphores(n_row, n_col):
+    outer = n_col // 2 if n_col % 2 == 0 else n_col
+    return [pltpu.SemaphoreType.DMA((n,)) for n in (outer, outer, outer, outer, n_row, n_row)]
+
+
+def in_vmem(n):
+    return [pl.BlockSpec(memory_space=pltpu.VMEM)] * n
+
+
+def gather(vectors, n_row, n_col, width):
+    vec = vectors.shape[0]
+    return pl.pallas_call(
+        functools.partial(gather_kernel, n_row, n_col),
+        out_shape=[jax.ShapeDtypeStruct((n * SB, vec, width), jnp.float32) for n in (n_col, n_row)],
+        in_specs=in_vmem(1),
+        out_specs=in_vmem(2),
+        scratch_shapes=[pltpu.VMEM((SB, vec, width), jnp.float32)] + semaphores(n_row, n_col),
+        compiler_params=pltpu.CompilerParams(
+            collective_id=0, has_side_effects=True, vmem_limit_bytes=16 * 2**20
+        ),
+    )(vectors)
+
+
+def scatter(direct, mirror, n_row, n_col):
+    _, vec, width = direct.shape
+    outer = n_col // 2 if n_col % 2 == 0 else n_col
+    slots = [pltpu.VMEM((n, SB, vec, width), jnp.float32) for n in (outer, outer, outer, n_row)]
+    return pl.pallas_call(
+        functools.partial(scatter_kernel, n_row, n_col),
+        out_shape=jax.ShapeDtypeStruct((vec, SB * width), jnp.float32),
+        in_specs=in_vmem(2),
+        out_specs=in_vmem(1)[0],
+        scratch_shapes=slots + semaphores(n_row, n_col),
+        compiler_params=pltpu.CompilerParams(
+            collective_id=1, has_side_effects=True, vmem_limit_bytes=16 * 2**20
+        ),
+    )(direct, mirror)
+
+
 def local(hamiltonian_blocks, block_vectors, row_list, col_list, counts):
     blocks = hamiltonian_blocks[0, 0]
-    vec, states = block_vectors.shape
-    width = blocks.shape[1]
-    own = block_vectors.reshape(vec, SB, width).transpose(1, 0, 2)
-    xr = lax.all_gather(own, "col", axis=0, tiled=True)
-    xc = lax.all_gather(own, "row", axis=0, tiled=True)
+    n_row = lax.axis_size("row")
+    n_col = lax.axis_size("col")
+    xr, xc = gather(block_vectors, n_row, n_col, blocks.shape[1])
     direct, mirror = products(blocks, xr, xc, row_list[0, 0], col_list[0, 0], counts[0])
-    total = lax.psum_scatter(direct, "col", scatter_dimension=0, tiled=True)
-    total = total + lax.psum_scatter(mirror, "row", scatter_dimension=0, tiled=True)
-    return total.transpose(1, 0, 2).reshape(vec, states)
+    return scatter(direct, mirror, n_row, n_col)
 
 
 def solution(mesh):

time: 161 us -> 47.6 us (0.30)
  waiting for transfers between devices: 90.2 us -> 0 us
  blocking collectives: 39.1 us -> 0 us
  Pallas kernels: 13.6 us -> 43.7 us
  between operations: 14.1 us -> 0.68 us
    reduce_scatter x2 -> x0, waiting for transfers between devices: 89.5 us -> none  [the longest x1 66.1 us: local(): total = lax.psum_scatter(direct, 'col', scatter_dimension=0, tiled=True)]
    all_gather x2 -> x0, blocking collectives: 39.1 us -> none  [the longest x1 31.9 us: local(): xr = lax.all_gather(own, 'col', axis=0, tiled=True)]
    pallas_call x0 -> x2, Pallas kernels: none -> 31 us  [the longest x1 16 us: gather(): pl.pallas_call(functools.partial(gather_kernel, n_row, n_col), out_shape=...]
  transfers between devices with their start and end apart: 2 -> 0, of which waited for: 2 -> 0; matrix products, arithmetic and copies ran while one was open for 0% -> 0% of each run, Pallas kernels for 0% -> 0%
where the time goes in v2:
time: 47.6 us; the launch traced here: 47.2 us
  Pallas kernels  43.7 us (92%)
  local copies, waits for them, and re-layouts  1.47 us (3%)
  other arithmetic  1.4 us (3%)
  between operations  0.68 us (1%)
    pallas_call x1, Pallas kernels, gather(): pl.pallas_call(functools.partial(gather_kernel, n_row, n_col), out_shape=...  16 us
    pallas_call x1, Pallas kernels, scatter(): pl.pallas_call(functools.partial(scatter_kernel, n_row, n_col), out_shape...  15 us
    pallas_call x1, Pallas kernels, products(): pl.pallas_call(functools.partial(products_kernel, chunk, unroll), grid_sp...  12.7 us
    unnamed x3, local copies, waits for them, and re-layouts  1.47 us
    unnamed x2, other arithmetic  1.4 us

profile of v2, /device:TPU:0, one launch (start us, length us, event | category | flops | bytes accessed | tf_op | source)
XLA Modules:
  0.0 47.2 jit_solution(10831063930415939589)
XLA Ops:
  0.7 0.7 %reduce.rows = s32[320]{0:T(512)S(1)} reduce(s32[1,1,320]{2,1,0:T(1,128)} %param.7, s32[]{:T(128)} %constant.4), dimensions={0,1}, to_apply=%param.7.reduce_sub_computation | reduce | bytes 2564 | tf_op args[2]
  1.4 0.7 %reduce.1.cols = s32[320]{0:T(512)S(1)} reduce(s32[1,1,320]{2,1,0:T(1,128)} %param.8, s32[]{:T(128)} %constant.4), dimensions={0,1}, to_apply=%param.8.reduce_sub_computation | reduce | bytes 2564 | tf_op args[3]
  2.1 0.0 copy-start
  2.1 0.8 %copy-done = f32[16,1024]{1,0:T(8,128)S(1)} copy-done((f32[16,1024]{1,0:T(8,128)S(1)}, f32[16,1024]{1,0:T(8,128)}, u32[]{:S(2)}) %copy-start) | copy-done | bytes 65560
  2.9 16.0 %shard_map.55 = (f32[64,16,128]{2,1,0:T(8,128)S(1)}, f32[32,16,128]{2,1,0:T(8,128)S(1)}) custom-call(f32[16,1024]{1,0:T(8,128)S(1)} %copy-done), custom_call_target="tpu_custom_call" | custom-call | tf_op jit(solution)/shard_map/pallas_call | solution.py:242
  18.9 12.7 %shard_map.56 = (f32[64,16,128]{2,1,0:T(8,128)S(1)}, f32[32,16,128]{2,1,0:T(8,128)S(1)}) custom-call(s32[320]{0:T(512)S(1)} %reduce.rows, s32[320]{0:T(512)S(1)} %reduce.1.cols, s32[1]{0:T(128)} %bitcast.2.counts, f32[320,128,128]{2,1,0:T(8,128)} %bitcast.3, f32[64,16,128]{2,1,0:T(8,128)S(1)} %get-tuple-element.9.xr, f32[32,16,128]{2,1,0:T(8,128)S(1)} %get-tuple-element.10.xc), custom_call_target="tpu_custom_call" | custom-call | tf_op jit(solution)/shard_map/pallas_call | solution.py:83
  31.6 15.0 %shard_map.57 = f32[16,1024]{1,0:T(8,128)S(1)} custom-call(f32[64,16,128]{2,1,0:T(8,128)S(1)} %get-tuple-element.11.direct, f32[32,16,128]{2,1,0:T(8,128)S(1)} %get-tuple-element.12.mirror), custom_call_target="tpu_custom_call" | custom-call | tf_op jit(solution)/shard_map/pallas_call | solution.py:258
  46.6 0.6 %copy.8 = f32[16,1024]{1,0:T(8,128)} copy(f32[16,1024]{1,0:T(8,128)S(1)} %shard_map.57) | data formatting | bytes 131072
Async XLA Ops:
  2.1 0.8 %copy-start = (f32[16,1024]{1,0:T(8,128)S(1)}, f32[16,1024]{1,0:T(8,128)}, u32[]{:S(2)}) copy-start(f32[16,1024]{1,0:T(8,128)} %vectors.1) | copy-start | bytes 196612

commit v3 on v2

--- a/solution.py
+++ b/solution.py
@@ -26,28 +26,30 @@
     lax.fori_loop(0, src.shape[0], body, 0)
 
 
-def products_kernel(chunk, unroll, rows, cols, counts, blocks, xr, xc, acc_d, acc_m, sr, sc):
-    step = pl.program_id(0)
+def products_kernel(group, rows, cols, counts, blocks, xr, xc, acc_d, acc_m, sr, sc, held, arrived):
     vec = xr.shape[1]
     width = xr.shape[2]
-
-    @pl.when(step == 0)
-    def _():
-        acc_d[...] = jnp.zeros_like(acc_d)
-        acc_m[...] = jnp.zeros_like(acc_m)
-        split_rows(xr, sr, vec)
-        split_rows(xc, sc, vec)
-
-    live = counts[0]
-
-    def group(g, _):
+    steps = held.shape[0] // group
+
+    def fetch(g):
+        part = pl.ds(g * group, group)
+        return pltpu.make_async_copy(blocks.at[part], held.at[part], arrived.at[g])
+
+    for g in range(steps):
+        fetch(g).start()
+    acc_d[...] = jnp.zeros_like(acc_d)
+    acc_m[...] = jnp.zeros_like(acc_m)
+    split_rows(xr, sr, vec)
+    split_rows(xc, sc, vec)
+    live = counts[0, 0]
+
+    def work(g):
         results = []
-        for u in range(unroll):
-            slot = g * unroll + u
-            k = step * chunk + slot
-            i = rows[k]
-            j = cols[k]
-            high, low = split(blocks[slot])
+        for u in range(group):
+            k = g * group + u
+            i = rows[0, 0, k]
+            j = cols[0, 0, k]
+            high, low = split(held[k])
             d = lax.dot_general(
                 sc[j],
                 jnp.concatenate([high, low], axis=0),
@@ -68,39 +70,36 @@
         for i, j, d, m in results:
             acc_d[i] = acc_d[i] + d
             acc_m[j] = acc_m[j] + m
+
+    def step(g, _):
+        fetch(g).wait()
+        pl.when(g * group < live)(lambda: work(g))
         return 0
 
-    groups = jnp.clip(pl.cdiv(live - step * chunk, unroll), 0, chunk // unroll)
-    lax.fori_loop(0, groups, group, 0)
+    lax.fori_loop(0, steps, step, 0)
 
 
 def products(blocks, xr, xc, rows, cols, counts):
     cap, width, _ = blocks.shape
     vec = xr.shape[1]
-    chunk = 32 if cap % 32 == 0 else cap
-    unroll = 8 if chunk % 8 == 0 else 1
-    whole = lambda shape: pl.BlockSpec(shape, lambda s, *_: (0, 0, 0))
+    group = next(n for n in (16, 8, 4, 2, 1) if cap % n == 0)
     return pl.pallas_call(
-        functools.partial(products_kernel, chunk, unroll),
-        grid_spec=pltpu.PrefetchScalarGridSpec(
-            num_scalar_prefetch=3,
-            grid=(cap // chunk,),
-            in_specs=[
-                pl.BlockSpec((chunk, width, width), lambda s, *_: (s, 0, 0)),
-                whole(xr.shape),
-                whole(xc.shape),
-            ],
-            out_specs=[whole(xr.shape), whole(xc.shape)],
-            scratch_shapes=[
-                pltpu.VMEM((xr.shape[0], 2 * vec, width), jnp.bfloat16),
-                pltpu.VMEM((xc.shape[0], 2 * vec, width), jnp.bfloat16),
-            ],
-        ),
+        functools.partial(products_kernel, group),
+        in_specs=[pl.BlockSpec(memory_space=pltpu.SMEM)] * 3
+        + [pl.BlockSpec(memory_space=pl.ANY)]
+        + in_vmem(2),
+        out_specs=in_vmem(2),
         out_shape=[
             jax.ShapeDtypeStruct(xr.shape, jnp.float32),
             jax.ShapeDtypeStruct(xc.shape, jnp.float32),
         ],
-        compiler_params=pltpu.CompilerParams(vmem_limit_bytes=40 * 2**20),
+        scratch_shapes=[
+            pltpu.VMEM((xr.shape[0], 2 * vec, width), jnp.bfloat16),
+            pltpu.VMEM((xc.shape[0], 2 * vec, width), jnp.bfloat16),
+            pltpu.VMEM(blocks.shape, jnp.float32),
+            pltpu.SemaphoreType.DMA((cap // group,)),
+        ],
+        compiler_params=pltpu.CompilerParams(vmem_limit_bytes=48 * 2**20),
     )(rows, cols, counts, blocks, xr, xc)
 
 
@@ -272,7 +271,7 @@
     n_row = lax.axis_size("row")
     n_col = lax.axis_size("col")
     xr, xc = gather(block_vectors, n_row, n_col, blocks.shape[1])
-    direct, mirror = products(blocks, xr, xc, row_list[0, 0], col_list[0, 0], counts[0])
+    direct, mirror = products(blocks, xr, xc, row_list, col_list, counts)
     return scatter(direct, mirror, n_row, n_col)
 
 

time: 47.6 us -> 42.4 us (0.89)
  Pallas kernels: 43.7 us -> 38.7 us
  other arithmetic: 1.4 us -> 0 us
  local copies, waits for them, and re-layouts: 1.47 us -> 2.82 us
    pallas_call x1, Pallas kernels: 12.7 us -> 7.74 us  [products(): pl.pallas_call(functools.partial(products_kernel, group), in_specs=[pl.Bl...]
    unnamed x2 -> x0, other arithmetic: 1.4 us -> none
    unnamed x3 -> x7, local copies, waits for them, and re-layouts: 1.47 us -> 2.82 us
where the time goes in v3:
time: 42.4 us; the launch traced here: 42.2 us
  Pallas kernels  38.7 us (91%)
  local copies, waits for them, and re-layouts  2.82 us (7%)
  between operations  0.69 us (2%)
    pallas_call x1, Pallas kernels, gather(): pl.pallas_call(functools.partial(gather_kernel, n_row, n_col), out_shape=...  16 us
    pallas_call x1, Pallas kernels, scatter(): pl.pallas_call(functools.partial(scatter_kernel, n_row, n_col), out_shape...  14.9 us
    pallas_call x1, Pallas kernels, products(): pl.pallas_call(functools.partial(products_kernel, group), in_specs=[pl.Bl...  7.74 us
    unnamed x7, local copies, waits for them, and re-layouts  2.82 us

profile of v3, /device:TPU:0, one launch (start us, length us, event | category | flops | bytes accessed | tf_op | source)
XLA Modules:
  0.0 42.2 jit_solution(7217987513556313173)
XLA Ops:
  0.7 0.0 copy-start
  0.7 0.8 %copy-done = f32[16,1024]{1,0:T(8,128)S(1)} copy-done((f32[16,1024]{1,0:T(8,128)S(1)}, f32[16,1024]{1,0:T(8,128)}, u32[]{:S(2)}) %copy-start) | copy-done | bytes 65560
  1.5 16.0 %shard_map.55 = (f32[64,16,128]{2,1,0:T(8,128)S(1)}, f32[32,16,128]{2,1,0:T(8,128)S(1)}) custom-call(f32[16,1024]{1,0:T(8,128)S(1)} %copy-done), custom_call_target="tpu_custom_call" | custom-call | tf_op jit(solution)/shard_map/pallas_call | solution.py:241
  17.5 0.0 copy-start.1
  17.5 0.7 %copy-done.1 = s32[1,1,320]{2,1,0:T(1,128)S(1)} copy-done((s32[1,1,320]{2,1,0:T(1,128)S(1)}, s32[1,1,320]{2,1,0:T(1,128)}, u32[]{:S(2)}) %copy-start.1) | copy-done | bytes 1304
  18.2 0.0 copy-start.2
  18.2 0.7 %copy-done.2 = s32[1,1,320]{2,1,0:T(1,128)S(1)} copy-done((s32[1,1,320]{2,1,0:T(1,128)S(1)}, s32[1,1,320]{2,1,0:T(1,128)}, u32[]{:S(2)}) %copy-start.2) | copy-done | bytes 1304
  18.9 7.7 %shard_map.56 = (f32[64,16,128]{2,1,0:T(8,128)S(1)}, f32[32,16,128]{2,1,0:T(8,128)S(1)}) custom-call(s32[1,1,320]{2,1,0:T(1,128)S(1)} %copy-done.1, s32[1,1,320]{2,1,0:T(1,128)S(1)} %copy-done.2, s32[1,1]{1,0:T(1,128)S(6)} %copy.7.counts, f32[320,128,128]{2,1,0:T(8,128)} %bitcast.1, f32[64,16,128]{2,1,0:T(8,128)S(1)} %get-tuple-element.9.xr, ...), custom_call_target="tpu_custom_call" | custom-call | tf_op jit(solution)/shard_map/pallas_call | solution.py:86
  26.6 14.9 %shard_map.57 = f32[16,1024]{1,0:T(8,128)S(1)} custom-call(f32[64,16,128]{2,1,0:T(8,128)S(1)} %get-tuple-element.11.direct, f32[32,16,128]{2,1,0:T(8,128)S(1)} %get-tuple-element.12.mirror), custom_call_target="tpu_custom_call" | custom-call | tf_op jit(solution)/shard_map/pallas_call | solution.py:257
  41.5 0.6 %copy.8 = f32[16,1024]{1,0:T(8,128)} copy(f32[16,1024]{1,0:T(8,128)S(1)} %shard_map.57) | data formatting | bytes 131072
Async XLA Ops:
  0.7 0.8 %copy-start = (f32[16,1024]{1,0:T(8,128)S(1)}, f32[16,1024]{1,0:T(8,128)}, u32[]{:S(2)}) copy-start(f32[16,1024]{1,0:T(8,128)} %vectors.1) | copy-start | bytes 196612
  17.5 0.7 %copy-start.1 = (s32[1,1,320]{2,1,0:T(1,128)S(1)}, s32[1,1,320]{2,1,0:T(1,128)}, u32[]{:S(2)}) copy-start(s32[1,1,320]{2,1,0:T(1,128)} %rows.1) | copy-start | bytes 3844
  18.2 0.7 %copy-start.2 = (s32[1,1,320]{2,1,0:T(1,128)S(1)}, s32[1,1,320]{2,1,0:T(1,128)}, u32[]{:S(2)}) copy-start(s32[1,1,320]{2,1,0:T(1,128)} %cols.1) | copy-start | bytes 3844

commit v4 on v3

--- a/solution.py
+++ b/solution.py
@@ -23,7 +23,7 @@
         dst[t, vec : 2 * vec, :] = low
         return 0
 
-    lax.fori_loop(0, src.shape[0], body, 0)
+    lax.fori_loop(0, src.shape[0], body, 0, unroll=8)
 
 
 def products_kernel(group, rows, cols, counts, blocks, xr, xc, acc_d, acc_m, sr, sc, held, arrived):

time: 42.4 us -> 42.4 us (level)
  no operation moved by 1% of the time
where the time goes in v4:
time: 42.4 us; the launch traced here: 42.3 us
  Pallas kernels  38.7 us (91%)
  local copies, waits for them, and re-layouts  2.82 us (7%)
  between operations  0.69 us (2%)
    pallas_call x1, Pallas kernels, gather(): pl.pallas_call(functools.partial(gather_kernel, n_row, n_col), out_shape=...  16 us
    pallas_call x1, Pallas kernels, scatter(): pl.pallas_call(functools.partial(scatter_kernel, n_row, n_col), out_shape...  15 us
    pallas_call x1, Pallas kernels, products(): pl.pallas_call(functools.partial(products_kernel, group), in_specs=[pl.Bl...  7.74 us
    unnamed x7, local copies, waits for them, and re-layouts  2.82 us

profile of v4, /device:TPU:0, one launch (start us, length us, event | category | flops | bytes accessed | tf_op | source)
XLA Modules:
  0.0 42.3 jit_solution(7805739493927153351)
XLA Ops:
  0.7 0.0 copy-start
  0.7 0.8 %copy-done = f32[16,1024]{1,0:T(8,128)S(1)} copy-done((f32[16,1024]{1,0:T(8,128)S(1)}, f32[16,1024]{1,0:T(8,128)}, u32[]{:S(2)}) %copy-start) | copy-done | bytes 65560
  1.5 16.0 %shard_map.55 = (f32[64,16,128]{2,1,0:T(8,128)S(1)}, f32[32,16,128]{2,1,0:T(8,128)S(1)}) custom-call(f32[16,1024]{1,0:T(8,128)S(1)} %copy-done), custom_call_target="tpu_custom_call" | custom-call | tf_op jit(solution)/shard_map/pallas_call | solution.py:241
  17.5 0.0 copy-start.1
  17.5 0.7 %copy-done.1 = s32[1,1,320]{2,1,0:T(1,128)S(1)} copy-done((s32[1,1,320]{2,1,0:T(1,128)S(1)}, s32[1,1,320]{2,1,0:T(1,128)}, u32[]{:S(2)}) %copy-start.1) | copy-done | bytes 1304
  18.2 0.0 copy-start.2
  18.2 0.7 %copy-done.2 = s32[1,1,320]{2,1,0:T(1,128)S(1)} copy-done((s32[1,1,320]{2,1,0:T(1,128)S(1)}, s32[1,1,320]{2,1,0:T(1,128)}, u32[]{:S(2)}) %copy-start.2) | copy-done | bytes 1304
  18.9 7.7 %shard_map.56 = (f32[64,16,128]{2,1,0:T(8,128)S(1)}, f32[32,16,128]{2,1,0:T(8,128)S(1)}) custom-call(s32[1,1,320]{2,1,0:T(1,128)S(1)} %copy-done.1, s32[1,1,320]{2,1,0:T(1,128)S(1)} %copy-done.2, s32[1,1]{1,0:T(1,128)S(6)} %copy.7.counts, f32[320,128,128]{2,1,0:T(8,128)} %bitcast.1, f32[64,16,128]{2,1,0:T(8,128)S(1)} %get-tuple-element.9.xr, ...), custom_call_target="tpu_custom_call" | custom-call | tf_op jit(solution)/shard_map/pallas_call | solution.py:86
  26.6 15.0 %shard_map.57 = f32[16,1024]{1,0:T(8,128)S(1)} custom-call(f32[64,16,128]{2,1,0:T(8,128)S(1)} %get-tuple-element.11.direct, f32[32,16,128]{2,1,0:T(8,128)S(1)} %get-tuple-element.12.mirror), custom_call_target="tpu_custom_call" | custom-call | tf_op jit(solution)/shard_map/pallas_call | solution.py:257
  41.6 0.6 %copy.8 = f32[16,1024]{1,0:T(8,128)} copy(f32[16,1024]{1,0:T(8,128)S(1)} %shard_map.57) | data formatting | bytes 131072
Async XLA Ops:
  0.7 0.8 %copy-start = (f32[16,1024]{1,0:T(8,128)S(1)}, f32[16,1024]{1,0:T(8,128)}, u32[]{:S(2)}) copy-start(f32[16,1024]{1,0:T(8,128)} %vectors.1) | copy-start | bytes 196612
  17.5 0.7 %copy-start.1 = (s32[1,1,320]{2,1,0:T(1,128)S(1)}, s32[1,1,320]{2,1,0:T(1,128)}, u32[]{:S(2)}) copy-start(s32[1,1,320]{2,1,0:T(1,128)} %rows.1) | copy-start | bytes 3844
  18.2 0.7 %copy-start.2 = (s32[1,1,320]{2,1,0:T(1,128)S(1)}, s32[1,1,320]{2,1,0:T(1,128)}, u32[]{:S(2)}) copy-start(s32[1,1,320]{2,1,0:T(1,128)} %cols.1) | copy-start | bytes 3844
